TPU v7x, 512 devices: a whole 4x8x8 slice. The times are simulated.
512 devices in a mesh: inst: 32 (over x, z), head: 16 (over y, core).
Axes of the slice: x: 4, y: 8, z: 8, core: 2. Of those that a mesh axis runs over, the one named last changes fastest.
Arguments:
- hidden_rows: bfloat16 [32, 32, 16, 9216], P('inst', None, None, 'head'), may hold values from -6 to 6
- send_counts: int32 [32, 32], P('inst'), may hold values from 0 to 16, as said below
- row_session: int32 [32, 32, 16], P('inst'), may hold values from 0 to 1, as said below
- row_position: int32 [32, 32, 16], P('inst'), may hold values from 0 to 1023, as said below
- resident_lengths: int32 [64], P('inst'), may hold values from 1 to 512, as said below
- kv_weight: bfloat16 [9216, 12288], P('inst', 'head'), may hold values from -0.0625 to 0.0625
- key_cache: bfloat16 [64, 1024, 6144], P('inst', None, 'head'), as said below
- value_cache: bfloat16 [64, 1024, 6144], P('inst', None, 'head'), may hold values from -6 to 6
- query: bfloat16 [64, 6144], P('inst', 'head'), as said below
- new_key: bfloat16 [64, 6144], P('inst', 'head'), may hold values from -6 to 6
- new_value: bfloat16 [64, 6144], P('inst', 'head'), may hold values from -6 to 6
Outputs:
- attended: bfloat16 [64, 6144], P('inst', 'head')
Inputs may be any that keep to these rules, and one draw needn't show every extreme that they name: `send_counts`: at most 16 live slots from one source to one destination; in every draw one destination instance receives 16 rows from every source. `row_session`: for a live slot, a session of the destination instance; 0 in slots that are not live. The destination that receives 16 rows from every source sends all of them to one of its sessions. `row_position`: the live rows of one destination session take each of the positions from its resident length to its resident length plus their number minus 1 exactly once; 0 in slots that are not live. In every draw some session's rows end at position 1023. `resident_lengths`: A session's resident length plus its restored rows stays within 1024 positions. `key_cache`: entries of order one. `query`: entries of order one or a few tens.
All inputs are finite; a program needn't handle non-finite values.
Results may differ from a plain program's by a relative error of at most 0.009.
Values may be sent and summed in bfloat16 or wider, within the bound.
No kernel may reach another device: no remote copies, remote signals or barrier semaphores. Data moves between devices by JAX's collectives and lax.ppermute only.
A program may use at most 192 MiB of HBM per device.

v0:
```python
import math
import jax
import jax.numpy as jnp
from jax import lax
from jax.sharding import PartitionSpec as P

HDIM = 128
masked_score = -1e30


def local(
    hidden_rows,
    send_counts,
    row_session,
    row_position,
    resident_lengths,
    kv_weight,
    key_cache,
    value_cache,
    query,
    new_key,
    new_value,
):
    sources = hidden_rows.shape[1]
    slot_cap = hidden_rows.shape[2]
    slot_count = sources * slot_cap
    head_dev = query.shape[1] // HDIM
    sessions_dev = key_cache.shape[0]
    context = key_cache.shape[1]
    inverse_root = 1.0 / math.sqrt(HDIM)
    arrived, counts_in, session_in, position_in = (
        lax.all_to_all(hidden_rows, "inst", split_axis=1, concat_axis=0, tiled=True),
        lax.all_to_all(send_counts, "inst", split_axis=1, concat_axis=0, tiled=True),
        lax.all_to_all(row_session, "inst", split_axis=1, concat_axis=0, tiled=True),
        lax.all_to_all(row_position, "inst", split_axis=1, concat_axis=0, tiled=True),
    )
    full_rows = lax.all_gather(
        arrived.reshape(slot_count, arrived.shape[3]), "head", axis=1, tiled=True
    )
    restored = jnp.dot(
        full_rows,
        lax.all_gather(kv_weight, "inst", axis=0, tiled=True),
        preferred_element_type=jnp.float32,
    )
    restored = restored.astype(jnp.bfloat16).reshape(slot_count, head_dev, 2, HDIM)
    restored_keys = restored[:, :, 0]
    restored_values = restored[:, :, 1]
    slot_live = (jnp.arange(slot_cap)[None, :] < counts_in).reshape(slot_count)
    session_map = session_in.reshape(slot_count)
    position_map = position_in.reshape(slot_count)
    member = (session_map[None, :] == jnp.arange(sessions_dev)[:, None]) & slot_live[None, :]
    queries = query.reshape(sessions_dev, head_dev, HDIM)
    cache_keys = key_cache.reshape(sessions_dev, context, head_dev, HDIM)
    cache_values = value_cache.reshape(sessions_dev, context, head_dev, HDIM)
    own_score = (
        jnp.sum(
            queries.astype(jnp.float32)
            * new_key.reshape(sessions_dev, head_dev, HDIM).astype(jnp.float32),
            axis=-1,
        )
        * inverse_root
    )
    fresh_value = new_value.reshape(sessions_dev, head_dev, HDIM).astype(jnp.float32)
    position_ids = jnp.arange(context)
    target = jnp.where(slot_live, position_map, context)
    key_rows = cache_keys.at[session_map, target].set(restored_keys, mode="drop")
    value_rows = cache_values.at[session_map, target].set(restored_values, mode="drop")
    totals = resident_lengths + jnp.sum(member.astype(jnp.int32), axis=1)
    scores = (
        jnp.einsum("shd,sphd->shp", queries, key_rows, preferred_element_type=jnp.float32)
        * inverse_root
    )
    scores = jnp.where((position_ids[None, :] < totals[:, None])[:, None, :], scores, masked_score)
    highest = jnp.maximum(jnp.max(scores, axis=-1), own_score)
    weights = jnp.exp(scores - highest[:, :, None])
    own_weight = jnp.exp(own_score - highest)
    denominator = jnp.sum(weights, axis=-1) + own_weight
    probability = (weights / denominator[:, :, None]).astype(jnp.bfloat16)
    attended = jnp.einsum(
        "shp,sphd->shd", probability, value_rows, preferred_element_type=jnp.float32
    )
    own_prob = (own_weight / denominator).astype(jnp.bfloat16)
    attended = attended + own_prob.astype(jnp.float32)[:, :, None] * fresh_value
    return attended.astype(jnp.bfloat16).reshape(sessions_dev, head_dev * HDIM)


def solution(mesh):
    placed = (
        P("inst", None, None, "head"),
        P("inst", None),
        P("inst", None, None),
        P("inst", None, None),
        P("inst"),
        P("inst", "head"),
        P("inst", None, "head"),
        P("inst", None, "head"),
        P("inst", "head"),
        P("inst", "head"),
        P("inst", "head"),
    )
    return jax.shard_map(
        local, mesh=mesh, in_specs=placed, out_specs=P("inst", "head"), check_vma=False
    )
```

profile of v0, /device:TPU:1, one launch (start us, length us, event | category | flops | bytes accessed | tf_op | source)
XLA Modules:
  0.0 339.8 jit_solution(13822352009684851430)
XLA Ops:
  6.6 30.2 %all_to_all.40 = bf16[1,32,16,576]{3,2,0,1:T(8,128)(2,1)S(1)} all-to-all(bf16[1,32,16,576]{3,2,0,1:T(8,128)(2,1)} %bitcast.46), channel_id=1, replica_groups=mesh['inst'=32,'head'=16] {'inst'}, dimensions={1} | all-to-all | bytes 1179648 | tf_op jit(solution)/shard_map/all_to_all | solution.py:32
  36.9 1.1 copy.77
  38.0 0.7 all-gather.5.cloned.1.call-update
  38.7 0.7 copy.73
  39.4 8.4 %all-to-all-start.1 = ((s32[1,32,1]{2,0,1:T(1,128)}), s32[1,32,1]{2,0,1:T(1,128)S(1)}, u32[]{:S(2)}, u32[]{:S(2)}) async-start(s32[1,32,1]{2,0,1:T(1,128)} %copy.73), calls=%async_computation.1 | async-start | bytes 32768 | tf_op jit(solution)/shard_map/all_to_all | solution.py:33
  47.9 0.7 copy.72
  48.5 7.9 %all-to-all-done.1 = s32[1,32,1]{2,0,1:T(1,128)S(1)} async-done(((s32[1,32,1]{2,0,1:T(1,128)}), s32[1,32,1]{2,0,1:T(1,128)S(1)}, u32[]{:S(2)}, u32[]{:S(2)}) %all-to-all-start.1) | async-done | bytes 160 | tf_op jit(solution)/shard_map/all_to_all | solution.py:33
  56.4 3.8 %all-to-all-start = ((s32[1,32,16]{2,0,1:T(1,128)}), s32[1,32,16]{2,0,1:T(1,128)S(1)}, u32[]{:S(2)}, u32[]{:S(2)}) async-start(s32[1,32,16]{2,0,1:T(1,128)} %copy.72), calls=%async_computation | async-start | bytes 32768 | tf_op jit(solution)/shard_map/all_to_all | solution.py:34
  60.4 0.7 copy.75
  61.1 0.7 copy.74
  61.9 2.6 copy.79
  64.5 0.7 copy.82
  65.3 2.6 copy.84
  67.9 0.7 reduce.1
  68.5 0.3 all-to-all-done
  68.8 9.1 %all-to-all-start.2 = ((s32[1,32,16]{2,0,1:T(1,128)}), s32[1,32,16]{2,0,1:T(1,128)S(1)}, u32[]{:S(2)}, u32[]{:S(2)}) async-start(s32[1,32,16]{2,0,1:T(1,128)} %copy.75), calls=%async_computation.2 | async-start | bytes 32768 | tf_op jit(solution)/shard_map/all_to_all | solution.py:35
  78.3 0.5 broadcast.131
  78.8 0.7 reduce.10
  79.6 6.8 %all-to-all-done.2 = s32[1,32,16]{2,0,1:T(1,128)S(1)} async-done(((s32[1,32,16]{2,0,1:T(1,128)}), s32[1,32,16]{2,0,1:T(1,128)S(1)}, u32[]{:S(2)}, u32[]{:S(2)}) %all-to-all-start.2) | async-done | bytes 2080 | tf_op jit(solution)/shard_map/all_to_all | solution.py:35
  86.4 0.7 reduce.9
  87.4 15.0 %all-gather.3.cloned.1.call-done = bf16[512,9216]{0,1:T(8,128)(2,1)} async-done(((bf16[512,576]{0,1:T(8,128)(2,1)}), bf16[512,9216]{0,1:T(8,128)(2,1)}) %all-gather.3.cloned.1.call-update) | async-done | bytes 9437200 | tf_op jit(solution)/shard_map/all_gather | solution.py:37
  102.4 135.1 %all-gather.5.cloned.1.call-done = bf16[9216,768]{1,0:T(8,128)(2,1)} async-done(((bf16[288,768]{1,0:T(8,128)(2,1)}), bf16[9216,768]{1,0:T(8,128)(2,1)}) %all-gather.5.cloned.1.call-update) | async-done | bytes 14155792 | tf_op jit(solution)/shard_map/all_gather | solution.py:42
  237.4 14.2 %convolution_convert_fusion = bf16[512,768]{1,0:T(8,128)(2,1)S(1)} fusion(bf16[512,9216]{0,1:T(8,128)(2,1)} %all-gather.3.cloned.1.call-done, bf16[9216,768]{1,0:T(8,128)(2,1)} %all-gather.5.cloned.1.call-done), kind=kOutput, calls=%fused_computation.6 | convolution fusion | flops 7248150528 | bytes 24379392 | tf_op jit(solution)/shard_map/dot_general | solution.py:40
  251.6 0.2 reshape.179
  251.8 1.1 fusion.15
  253.1 0.3 copy.85
  253.4 0.3 copy.80
  253.8 55.4 %scatter_fusion = bf16[2,1024,3,128]{3,2,1,0:T(4,128)(2,1)} fusion(bf16[2,1024,3,128]{3,2,1,0:T(4,128)(2,1)} %copy.79, s32[512]{0:T(512)S(1)} %bitcast.41, bf16[512,3,128]{2,1,0:T(4,128)(2,1)S(1)} %copy.80), kind=kCustom, calls=%fused_computation | custom fusion | bytes 1183744 | tf_op jit(solution)/shard_map/scatter | solution.py:66
  309.2 2.1 fusion.2
  311.8 20.1 %scatter_fusion.1 = bf16[2,1024,3,128]{3,2,1,0:T(4,128)(2,1)S(1)} fusion(bf16[2,1024,3,128]{3,2,1,0:T(4,128)(2,1)S(1)} %copy-done, s32[512]{0:T(512)S(1)} %bitcast.42, bf16[512,3,128]{2,1,0:T(4,128)(2,1)S(1)} %copy.85), kind=kCustom, calls=%fused_computation.1 | custom fusion | bytes 1183744 | tf_op jit(solution)/shard_map/scatter | solution.py:67
  331.9 0.4 fusion
  332.3 0.6 copy.115
  (47 shorter events, 1.8 us)
Async XLA Ops:
  6.5 32.2 %copy-start.8 = (s32[1,32]{1,0:T(1,128)S(1)}, s32[1,32]{1,0:T(1,128)}, u32[]{:S(2)}) copy-start(s32[1,32]{1,0:T(1,128)} %param.12) | copy-start | bytes 388
  6.5 41.3 %copy-start.5 = (bf16[2,384]{1,0:T(2,128)(2,1)S(1)}, bf16[2,384]{1,0:T(2,128)(2,1)}, u32[]{:S(2)}) copy-start(bf16[2,384]{1,0:T(2,128)(2,1)} %param.19) | copy-start | bytes 4612
  6.5 41.3 %copy-start.6 = (bf16[2,384]{1,0:T(2,128)(2,1)S(1)}, bf16[2,384]{1,0:T(2,128)(2,1)}, u32[]{:S(2)}) copy-start(bf16[2,384]{1,0:T(2,128)(2,1)} %param.20) | copy-start | bytes 4612
  6.5 41.3 %copy-start.3 = (s32[1,32,16]{1,2,0:T(8,128)S(1)}, s32[1,32,16]{1,2,0:T(8,128)}, u32[]{:S(2)}) copy-start(s32[1,32,16]{1,2,0:T(8,128)} %param.13) | copy-start | bytes 6148
  6.5 53.9 %copy-start.7 = (bf16[2,384]{1,0:T(2,128)(2,1)S(1)}, bf16[2,384]{1,0:T(2,128)(2,1)}, u32[]{:S(2)}) copy-start(bf16[2,384]{1,0:T(2,128)(2,1)} %param.21) | copy-start | bytes 4612
  6.5 53.9 %copy-start.4 = (s32[1,32,16]{1,2,0:T(8,128)S(1)}, s32[1,32,16]{1,2,0:T(8,128)}, u32[]{:S(2)}) copy-start(s32[1,32,16]{1,2,0:T(8,128)} %param.14) | copy-start | bytes 6148
  6.6 54.5 %copy-start.1 = (bf16[2,1024,384]{2,1,0:T(8,128)(2,1)S(1)}, bf16[2,1024,384]{2,1,0:T(8,128)(2,1)}, u32[]{:S(2)}) copy-start(bf16[2,1024,384]{2,1,0:T(8,128)(2,1)} %param.17) | copy-start | bytes 4718596
  6.6 95.8 %all-gather.3.cloned.1.call-start = ((), (), s32[]{:S(2)}) async-start(), calls=%async_computation.4 | async-start | bytes 10027008 | tf_op jit(solution)/shard_map/all_gather | solution.py:37
  37.9 199.5 %all-gather.5.cloned.1.call-start = ((), (), s32[]{:S(2)}) async-start(), calls=%async_computation.5 | async-start | bytes 14598144 | tf_op jit(solution)/shard_map/all_gather | solution.py:42
  39.4 17.0 %all-to-all-start.1 = ((s32[1,32,1]{2,0,1:T(1,128)}), s32[1,32,1]{2,0,1:T(1,128)S(1)}, u32[]{:S(2)}, u32[]{:S(2)}) async-start(s32[1,32,1]{2,0,1:T(1,128)} %copy.73), calls=%async_computation.1 | async-start | bytes 32768 | tf_op jit(solution)/shard_map/all_to_all | solution.py:33
  56.4 12.4 %all-to-all-start = ((s32[1,32,16]{2,0,1:T(1,128)}), s32[1,32,16]{2,0,1:T(1,128)S(1)}, u32[]{:S(2)}, u32[]{:S(2)}) async-start(s32[1,32,16]{2,0,1:T(1,128)} %copy.72), calls=%async_computation | async-start | bytes 32768 | tf_op jit(solution)/shard_map/all_to_all | solution.py:34
  61.9 2.6 copy-start.2
  65.3 22.0 %copy-start.9 = (s32[2]{0:T(128)S(1)}, s32[2]{0:T(128)}, u32[]{:S(2)}) copy-start(s32[2]{0:T(128)} %param.15) | copy-start | bytes 28
  68.8 17.6 %all-to-all-start.2 = ((s32[1,32,16]{2,0,1:T(1,128)}), s32[1,32,16]{2,0,1:T(1,128)S(1)}, u32[]{:S(2)}, u32[]{:S(2)}) async-start(s32[1,32,16]{2,0,1:T(1,128)} %copy.75), calls=%async_computation.2 | async-start | bytes 32768 | tf_op jit(solution)/shard_map/all_to_all | solution.py:35
  253.8 58.1 %copy-start = (bf16[2,1024,3,128]{3,2,1,0:T(4,128)(2,1)S(1)}, bf16[2,1024,3,128]{3,2,1,0:T(4,128)(2,1)}, u32[]{:S(2)}) copy-start(bf16[2,1024,3,128]{3,2,1,0:T(4,128)(2,1)} %copy.84) | copy-start | bytes 4718596
Sparse Core Ops, SparseCore 0:
  38.1 64.2 all-gather.2
  105.5 131.8 all-gather.4
where the time goes:
time: 341 us; the launch traced here: 340 us
  waiting for transfers between devices  166 us (49%)
  local copies, waits for them, and re-layouts  89.2 us (26%)
  blocking collectives  30.2 us (9%)
  starting transfers between devices  21.4 us (6%)
  matrix products  16.6 us (5%)
  between operations  13.6 us (4%)
    all_gather x1, waiting for transfers between devices, local(): lax.all_gather(kv_weight, 'inst', axis=0, tiled=True)  135 us
    scatter x1, local copies, waits for them, and re-layouts, local(): cache_keys.at[session_map, target].set(restored_keys, mode='drop')  55.4 us
    all_to_all x1, blocking collectives, local(): lax.all_to_all(hidden_rows, 'inst', split_axis=1, concat_axis=0, tiled=True)  30.2 us
    scatter x1, local copies, waits for them, and re-layouts, local(): cache_values.at[session_map, target].set(restored_values, mode='drop')  20.1 us
    all_gather x1, waiting for transfers between devices, local(): lax.all_gather(arrived.reshape(slot_count, arrived.shape[3]), 'head', axi...  15 us
    dot_general x1, matrix products, local(): jnp.dot(full_rows, lax.all_gather(kv_weight, 'inst', axis=0, tiled=True),...  14.2 us
    all_to_all x1, starting transfers between devices, local(): lax.all_to_all(row_position, 'inst', split_axis=1, concat_axis=0, tiled=T...  9.1 us
    all_to_all x1, starting transfers between devices, local(): lax.all_to_all(send_counts, 'inst', split_axis=1, concat_axis=0, tiled=True)  8.39 us
  transfers between devices with their start and end apart: 5, of which 5 were waited for; matrix products, arithmetic and copies ran while one was open for 4% of the time, Pallas kernels for 0%

commit v1 on v0

--- a/solution.py
+++ b/solution.py
@@ -6,6 +6,12 @@
 
 HDIM = 128
 masked_score = -1e30
+
+
+def swap_blocks(array, name, split, join):
+    parts = jnp.split(array, lax.axis_size(name), axis=split)
+    incoming = lax.all_to_all(jnp.stack(parts), name, 0, 0)
+    return jnp.concatenate(incoming, axis=join)
 
 
 def local(
@@ -32,7 +38,7 @@
         lax.all_to_all(hidden_rows, "inst", split_axis=1, concat_axis=0, tiled=True),
         lax.all_to_all(send_counts, "inst", split_axis=1, concat_axis=0, tiled=True),
         lax.all_to_all(row_session, "inst", split_axis=1, concat_axis=0, tiled=True),
-        lax.all_to_all(row_position, "inst", split_axis=1, concat_axis=0, tiled=True),
+        swap_blocks(row_position, "inst", 1, 0),
     )
     full_rows = lax.all_gather(
         arrived.reshape(slot_count, arrived.shape[3]), "head", axis=1, tiled=True

time: 341 us -> 341 us (level)
  waiting for transfers between devices: 166 us -> 143 us
  local copies, waits for them, and re-layouts: 89.2 us -> 107 us
  starting transfers between devices: 21.4 us -> 26.8 us
    unnamed x25 -> x55, local copies, waits for them, and re-layouts: 3.47 us -> 19.7 us
    all_gather x1, waiting for transfers between devices: 15 us -> 0.02 us  [local(): lax.all_gather(arrived.reshape(slot_count, arrived.shape[3]), 'head', axi...]
    all_to_all x1, waiting for transfers between devices: 7.89 us -> 0.01 us  [local(): lax.all_to_all(send_counts, 'inst', split_axis=1, concat_axis=0, tiled=True)]
    all_to_all x1, waiting for transfers between devices: 0.32 us -> 6.91 us  [local(): lax.all_to_all(row_session, 'inst', split_axis=1, concat_axis=0, tiled=True)]
    all_to_all x1, waiting for transfers between devices: 6.81 us -> 0.3 us  [swap_blocks(): incoming = lax.all_to_all(jnp.stack(parts), name, 0, 0)]
    all_to_all x1, starting transfers between devices: 3.78 us -> 9.13 us  [local(): lax.all_to_all(row_session, 'inst', split_axis=1, concat_axis=0, tiled=True)]
  transfers between devices with their start and end apart: 5 -> 5, of which waited for: 5 -> 3; matrix products, arithmetic and copies ran while one was open for 4% -> 9% of each run, Pallas kernels for 0% -> 0%
where the time goes in v1:
time: 341 us; the launch traced here: 339 us
  waiting for transfers between devices  143 us (42%)
  local copies, waits for them, and re-layouts  107 us (31%)
  blocking collectives  30.2 us (9%)
  starting transfers between devices  26.8 us (8%)
  matrix products  16.6 us (5%)
  between operations  13.6 us (4%)
    all_gather x1, waiting for transfers between devices, local(): lax.all_gather(kv_weight, 'inst', axis=0, tiled=True)  135 us
    scatter x1, local copies, waits for them, and re-layouts, local(): cache_keys.at[session_map, target].set(restored_keys, mode='drop')  55.1 us
    all_to_all x1, blocking collectives, local(): lax.all_to_all(hidden_rows, 'inst', split_axis=1, concat_axis=0, tiled=True)  30.2 us
    scatter x1, local copies, waits for them, and re-layouts, local(): cache_values.at[session_map, target].set(restored_values, mode='drop')  20.1 us
    unnamed x55, local copies, waits for them, and re-layouts  19.7 us
    dot_general x1, matrix products, local(): jnp.dot(full_rows, lax.all_gather(kv_weight, 'inst', axis=0, tiled=True),...  14.2 us
    all_to_all x1, starting transfers between devices, swap_blocks(): incoming = lax.all_to_all(jnp.stack(parts), name, 0, 0)  9.24 us
    all_to_all x1, starting transfers between devices, local(): lax.all_to_all(row_session, 'inst', split_axis=1, concat_axis=0, tiled=True)  9.13 us
  transfers between devices with their start and end apart: 5, of which 3 were waited for; matrix products, arithmetic and copies ran while one was open for 9% of the time, Pallas kernels for 0%

profile of v1, /device:TPU:1, one launch (start us, length us, event | category | flops | bytes accessed | tf_op | source)
XLA Modules:
  0.0 339.5 jit_solution(10518289951586894548)
XLA Ops:
  6.6 30.2 %all_to_all.36 = bf16[1,32,16,576]{3,2,0,1:T(8,128)(2,1)S(1)} all-to-all(bf16[1,32,16,576]{3,2,0,1:T(8,128)(2,1)} %bitcast.109), channel_id=1, replica_groups=mesh['inst'=32,'head'=16] {'inst'}, dimensions={1} | all-to-all | bytes 1179648 | tf_op jit(solution)/shard_map/all_to_all | solution.py:38
  36.9 1.1 copy.71
  38.0 0.7 all-gather.5.cloned.1.call-update
  38.7 0.7 copy.68
  39.4 8.4 %all-to-all-start.1 = ((s32[1,32,1]{2,0,1:T(1,128)}), s32[1,32,1]{2,0,1:T(1,128)S(1)}, u32[]{:S(2)}, u32[]{:S(2)}) async-start(s32[1,32,1]{2,0,1:T(1,128)} %copy.68), calls=%async_computation.1 | async-start | bytes 32768 | tf_op jit(solution)/shard_map/all_to_all | solution.py:39
  51.4 0.6 constant_dynamic-update-slice_fusion.26
  52.5 0.6 constant_dynamic-update-slice_fusion.24
  55.7 0.6 constant_dynamic-update-slice_fusion.18
  57.4 0.6 constant_dynamic-update-slice_fusion.15
  58.0 0.6 constant_dynamic-update-slice_fusion.14
  59.1 0.6 constant_dynamic-update-slice_fusion.12
  61.8 0.6 constant_dynamic-update-slice_fusion.7
  62.9 0.6 constant_dynamic-update-slice_fusion.5
  63.5 0.6 constant_dynamic-update-slice_fusion.4
  66.2 9.2 %all-to-all-start.2 = ((s32[32,1,1,16]{3,2,1,0:T(1,128)}), s32[32,1,1,16]{3,2,1,0:T(1,128)S(1)}, u32[]{:S(2)}, u32[]{:S(2)}) async-start(s32[32,1,1,16]{3,2,1,0:T(1,128)} %constant_dynamic-update-slice_fusion), calls=%async_computation.2 | async-start | bytes 32768 | tf_op jit(solution)/shard_map/all_to_all | solution.py:13
  75.7 0.7 copy.67
  76.4 0.7 copy.69
  77.1 2.6 copy.73
  79.8 0.7 copy.76
  80.6 2.6 copy.78
  83.2 0.7 reduce.1
  84.1 9.1 %all-to-all-start = ((s32[1,32,16]{2,0,1:T(1,128)}), s32[1,32,16]{2,0,1:T(1,128)S(1)}, u32[]{:S(2)}, u32[]{:S(2)}) async-start(s32[1,32,16]{2,0,1:T(1,128)} %copy.67), calls=%async_computation | async-start | bytes 32768 | tf_op jit(solution)/shard_map/all_to_all | solution.py:40
  94.0 0.7 reduce.73
  94.8 6.9 %all-to-all-done = s32[1,32,16]{2,0,1:T(1,128)S(1)} async-done(((s32[1,32,16]{2,0,1:T(1,128)}), s32[1,32,16]{2,0,1:T(1,128)S(1)}, u32[]{:S(2)}, u32[]{:S(2)}) %all-to-all-start) | async-done | bytes 2080 | tf_op jit(solution)/shard_map/all_to_all | solution.py:40
  101.8 0.7 reduce.74
  102.8 134.6 %all-gather.5.cloned.1.call-done = bf16[9216,768]{1,0:T(8,128)(2,1)} async-done(((bf16[288,768]{1,0:T(8,128)(2,1)}), bf16[9216,768]{1,0:T(8,128)(2,1)}) %all-gather.5.cloned.1.call-update) | async-done | bytes 14155792 | tf_op jit(solution)/shard_map/all_gather | solution.py:48
  237.5 14.2 %convolution_convert_fusion = bf16[512,768]{1,0:T(8,128)(2,1)S(1)} fusion(bf16[512,9216]{0,1:T(8,128)(2,1)} %all-gather.3.cloned.1.call-done, bf16[9216,768]{1,0:T(8,128)(2,1)} %all-gather.5.cloned.1.call-done), kind=kOutput, calls=%fused_computation.6 | convolution fusion | flops 7248150528 | bytes 24379392 | tf_op jit(solution)/shard_map/dot_general | solution.py:46
  251.8 1.1 fusion.15
  253.8 55.1 %scatter_fusion = bf16[2,1024,3,128]{3,2,1,0:T(4,128)(2,1)} fusion(bf16[2,1024,3,128]{3,2,1,0:T(4,128)(2,1)} %copy.73, s32[512]{0:T(512)S(1)} %bitcast.104, bf16[512,3,128]{2,1,0:T(4,128)(2,1)S(1)} %copy.74), kind=kCustom, calls=%fused_computation | custom fusion | bytes 1183744 | tf_op jit(solution)/shard_map/scatter | solution.py:72
  308.9 2.1 fusion.2
  311.5 20.1 %scatter_fusion.1 = bf16[2,1024,3,128]{3,2,1,0:T(4,128)(2,1)S(1)} fusion(bf16[2,1024,3,128]{3,2,1,0:T(4,128)(2,1)S(1)} %copy-done.1, s32[512]{0:T(512)S(1)} %bitcast.105, bf16[512,3,128]{2,1,0:T(4,128)(2,1)S(1)} %copy.79), kind=kCustom, calls=%fused_computation.1 | custom fusion | bytes 1183744 | tf_op jit(solution)/shard_map/scatter | solution.py:73
  332.1 0.6 copy.109
  (80 shorter events, 17.0 us)
Async XLA Ops:
  6.5 32.2 %copy-start.8 = (s32[1,32]{1,0:T(1,128)S(1)}, s32[1,32]{1,0:T(1,128)}, u32[]{:S(2)}) copy-start(s32[1,32]{1,0:T(1,128)} %param.12) | copy-start | bytes 388
  6.5 41.3 %copy-start = (s32[1,32,16]{1,2,0:T(8,128)S(1)}, s32[1,32,16]{1,2,0:T(8,128)}, u32[]{:S(2)}) copy-start(s32[1,32,16]{1,2,0:T(8,128)} %param.14) | copy-start | bytes 6148
  6.5 59.6 %copy-start.5 = (bf16[2,384]{1,0:T(2,128)(2,1)S(1)}, bf16[2,384]{1,0:T(2,128)(2,1)}, u32[]{:S(2)}) copy-start(bf16[2,384]{1,0:T(2,128)(2,1)} %param.19) | copy-start | bytes 4612
  6.5 59.7 %copy-start.6 = (bf16[2,384]{1,0:T(2,128)(2,1)S(1)}, bf16[2,384]{1,0:T(2,128)(2,1)}, u32[]{:S(2)}) copy-start(bf16[2,384]{1,0:T(2,128)(2,1)} %param.20) | copy-start | bytes 4612
  6.5 69.1 %copy-start.7 = (bf16[2,384]{1,0:T(2,128)(2,1)S(1)}, bf16[2,384]{1,0:T(2,128)(2,1)}, u32[]{:S(2)}) copy-start(bf16[2,384]{1,0:T(2,128)(2,1)} %param.21) | copy-start | bytes 4612
  6.5 69.1 %copy-start.4 = (s32[1,32,16]{1,2,0:T(8,128)S(1)}, s32[1,32,16]{1,2,0:T(8,128)}, u32[]{:S(2)}) copy-start(s32[1,32,16]{1,2,0:T(8,128)} %param.13) | copy-start | bytes 6148
  6.6 69.8 %copy-start.2 = (bf16[2,1024,384]{2,1,0:T(8,128)(2,1)S(1)}, bf16[2,1024,384]{2,1,0:T(8,128)(2,1)}, u32[]{:S(2)}) copy-start(bf16[2,1024,384]{2,1,0:T(8,128)(2,1)} %param.17) | copy-start | bytes 4718596
  6.6 96.2 %all-gather.3.cloned.1.call-start = ((), (), s32[]{:S(2)}) async-start(), calls=%async_computation.4 | async-start | bytes 10027008 | tf_op jit(solution)/shard_map/all_gather | solution.py:43
  38.0 199.5 %all-gather.5.cloned.1.call-start = ((), (), s32[]{:S(2)}) async-start(), calls=%async_computation.5 | async-start | bytes 14598144 | tf_op jit(solution)/shard_map/all_gather | solution.py:48
  39.4 26.8 %all-to-all-start.1 = ((s32[1,32,1]{2,0,1:T(1,128)}), s32[1,32,1]{2,0,1:T(1,128)S(1)}, u32[]{:S(2)}, u32[]{:S(2)}) async-start(s32[1,32,1]{2,0,1:T(1,128)} %copy.68), calls=%async_computation.1 | async-start | bytes 32768 | tf_op jit(solution)/shard_map/all_to_all | solution.py:39
  66.2 17.9 %all-to-all-start.2 = ((s32[32,1,1,16]{3,2,1,0:T(1,128)}), s32[32,1,1,16]{3,2,1,0:T(1,128)S(1)}, u32[]{:S(2)}, u32[]{:S(2)}) async-start(s32[32,1,1,16]{3,2,1,0:T(1,128)} %constant_dynamic-update-slice_fusion), calls=%async_computation.2 | async-start | bytes 32768 | tf_op jit(solution)/shard_map/all_to_all | solution.py:13
  77.1 2.6 copy-start.3
  80.5 22.1 %copy-start.9 = (s32[2]{0:T(128)S(1)}, s32[2]{0:T(128)}, u32[]{:S(2)}) copy-start(s32[2]{0:T(128)} %param.15) | copy-start | bytes 28
  84.1 17.6 %all-to-all-start = ((s32[1,32,16]{2,0,1:T(1,128)}), s32[1,32,16]{2,0,1:T(1,128)S(1)}, u32[]{:S(2)}, u32[]{:S(2)}) async-start(s32[1,32,16]{2,0,1:T(1,128)} %copy.67), calls=%async_computation | async-start | bytes 32768 | tf_op jit(solution)/shard_map/all_to_all | solution.py:40
  253.8 57.8 %copy-start.1 = (bf16[2,1024,3,128]{3,2,1,0:T(4,128)(2,1)S(1)}, bf16[2,1024,3,128]{3,2,1,0:T(4,128)(2,1)}, u32[]{:S(2)}) copy-start(bf16[2,1024,3,128]{3,2,1,0:T(4,128)(2,1)} %copy.78) | copy-start | bytes 4718596
Sparse Core Ops, SparseCore 0:
  38.1 64.2 all-gather.2
  105.5 131.8 all-gather.4
